TPU v7x, 32 devices: a whole 2x2x4 slice. The times are simulated.
32 devices in a mesh: group: 1, row: 32 (over z, y, x, core), col: 1.
Axes of the slice: x: 2, y: 2, z: 4, core: 2. Of those that a mesh axis runs over, the one named last changes fastest.
Arguments:
- field: bfloat16 [1280, 32, 8192], P(('group', 'row'), None, 'col'), may hold values from -6 to 6
- spec_weight: bfloat16 [2, 128, 32, 32, 128], P(None, 'row', None, None, 'col'), may hold values from -0.75 to 0.75
- point_weight: bfloat16 [32, 32], replicated, may hold values from -1 to 1
- bias: float32 [32], replicated, may hold values from -3 to 3
Outputs:
- output: bfloat16 [1280, 32, 8192], P(('group', 'row'), None, 'col')
All inputs are finite; a program needn't handle non-finite values.
Results may differ from a plain program's by a relative error of at most 0.0059.
Values may be sent and summed in bfloat16 or wider, within the bound.
A program may use at most 128 MiB of HBM per device.

v0:
```python
import math

import jax
import jax.numpy as jnp
from jax import lax
from jax.sharding import PartitionSpec as P


def forward_columns(y_global, modes_y, length_y):
    freq = jnp.arange(modes_y, dtype=jnp.int32)
    phase = (y_global[:, None] * freq[None, :] % length_y).astype(jnp.float32) * (
        2.0 * math.pi / length_y
    )
    scale = 1.0 / math.sqrt(length_y)
    return jnp.concatenate([jnp.cos(phase) * scale, -jnp.sin(phase) * scale], axis=1).astype(
        jnp.bfloat16
    )


def row_phase(x_global, modes_x, length_x):
    index = jnp.arange(modes_x, dtype=jnp.int32)
    freq = jnp.where(index < modes_x // 2, index, index - modes_x + length_x)
    return (freq[:, None] * x_global[None, :] % length_x).astype(jnp.float32) * (
        2.0 * math.pi / length_x
    )


def forward_rows(x_global, modes_x, length_x):
    phase = row_phase(x_global, modes_x, length_x)
    scale = 1.0 / math.sqrt(length_x)
    return (jnp.cos(phase) * scale, jnp.sin(phase) * scale)


def inverse_row_tables(x_global, modes_x, length_x):
    phase = row_phase(x_global, modes_x, length_x).T
    return (jnp.cos(phase).astype(jnp.bfloat16), jnp.sin(phase).astype(jnp.bfloat16))


def inverse_columns(y_global, modes_y, modes_x, length_y):
    freq = jnp.arange(modes_y, dtype=jnp.int32)
    phase = (freq[:, None] * y_global[None, :] % length_y).astype(jnp.float32) * (
        2.0 * math.pi / length_y
    )
    factor = jnp.where(freq == 0, 1.0, 2.0).astype(jnp.float32)[:, None] / math.sqrt(
        2.0 * modes_x * modes_y
    )
    return jnp.concatenate([factor * jnp.cos(phase), -factor * jnp.sin(phase)], axis=0).astype(
        jnp.bfloat16
    )


def row_section(partial_value, cosine, sine):
    highest = lax.Precision.HIGHEST
    real_part = partial_value[:, :, 0]
    imag_part = partial_value[:, :, 1]
    out_real = jnp.einsum("jx,xck->jck", cosine, real_part, precision=highest) + jnp.einsum(
        "jx,xck->jck", sine, imag_part, precision=highest
    )
    out_imag = jnp.einsum("jx,xck->jck", cosine, imag_part, precision=highest) - jnp.einsum(
        "jx,xck->jck", sine, real_part, precision=highest
    )
    return jnp.stack([out_real, out_imag])


def mix_modes(spectrum, spec_weight):
    weights = spec_weight.astype(jnp.float32)
    highest = lax.Precision.HIGHEST
    spec_real = spectrum[0]
    spec_imag = spectrum[1]
    out_real = jnp.einsum("jik,jiok->jok", spec_real, weights[0], precision=highest) - jnp.einsum(
        "jik,jiok->jok", spec_imag, weights[1], precision=highest
    )
    out_imag = jnp.einsum("jik,jiok->jok", spec_real, weights[1], precision=highest) + jnp.einsum(
        "jik,jiok->jok", spec_imag, weights[0], precision=highest
    )
    return jnp.stack([out_real, out_imag]).astype(jnp.bfloat16)


def invert_rows(mixed, inv_cos, inv_sin):
    half_real = jnp.einsum(
        "xj,jok->xok", inv_cos, mixed[0], preferred_element_type=jnp.float32
    ) - jnp.einsum("xj,jok->xok", inv_sin, mixed[1], preferred_element_type=jnp.float32)
    half_imag = jnp.einsum(
        "xj,jok->xok", inv_sin, mixed[0], preferred_element_type=jnp.float32
    ) + jnp.einsum("xj,jok->xok", inv_cos, mixed[1], preferred_element_type=jnp.float32)
    return jnp.stack([half_real, half_imag], axis=2).astype(jnp.bfloat16)


def shards(field, spec_weight, point_weight, bias):
    row_count, chan_count, col_count = field.shape
    row_devices = lax.axis_size("row")
    col_devices = lax.axis_size("col")
    row_index = lax.axis_index("row")
    col_index = lax.axis_index("col")
    block_x = spec_weight.shape[1]
    block_y = spec_weight.shape[4]
    modes_x = block_x * row_devices
    modes_y = block_y * col_devices
    length_x = row_count * row_devices
    length_y = col_count * col_devices
    x_global = row_index * row_count + jnp.arange(row_count, dtype=jnp.int32)
    y_global = col_index * col_count + jnp.arange(col_count, dtype=jnp.int32)
    table_y = forward_columns(y_global, modes_y, length_y)
    partial_value = jnp.dot(
        field.reshape(row_count * chan_count, col_count),
        table_y,
        preferred_element_type=jnp.float32,
    )
    partial_value = partial_value.reshape(row_count, chan_count, 2, modes_y)
    cosine, sine = forward_rows(x_global, modes_x, length_x)
    spectrum = lax.psum(row_section(partial_value, cosine, sine), ("row", "col"))
    zero = jnp.zeros((), jnp.int32)
    own_block = lax.dynamic_slice(
        spectrum,
        (zero, row_index * block_x, zero, col_index * block_y),
        (2, block_x, chan_count, block_y),
    )
    mixed = mix_modes(own_block, spec_weight)
    inv_cos, inv_sin = inverse_row_tables(x_global, modes_x, length_x)
    gathered = lax.all_gather(mixed[None], ("row", "col"), axis=0, tiled=True)
    gathered = gathered.reshape(row_devices, col_devices, 2, block_x, chan_count, block_y)
    gathered = gathered.transpose(2, 0, 3, 4, 1, 5).reshape(2, modes_x, chan_count, modes_y)
    inverse_half = invert_rows(gathered, inv_cos, inv_sin)
    table_back = inverse_columns(y_global, modes_y, modes_x, length_y)
    spectral = jnp.dot(
        inverse_half.reshape(row_count * chan_count, 2 * modes_y),
        table_back,
        preferred_element_type=jnp.float32,
    )
    spectral = spectral.reshape(row_count, chan_count, col_count)
    pointwise = jnp.einsum("oi,xiy->xoy", point_weight, field, preferred_element_type=jnp.float32)
    total = spectral + pointwise + bias[None, :, None]
    return jax.nn.gelu(total, approximate=True).astype(jnp.bfloat16)


def solution(mesh):
    placed = (P(("group", "row"), None, "col"), P(None, "row", None, None, "col"), P(), P())
    return jax.shard_map(
        shards,
        mesh=mesh,
        in_specs=placed,
        out_specs=P(("group", "row"), None, "col"),
        check_vma=False,
    )
```

profile of v0, /device:TPU:0, one launch (start us, length us, event | category | flops | bytes accessed | tf_op | source)
XLA Modules:
  0.0 320.4 jit_solution(264804710884545805)
XLA Ops:
  6.5 0.0 copy-start
  6.5 0.0 all-reduce.2.cloned.1.call-start
  6.5 18.0 %multiply_convert_fusion.2 = (bf16[8192,128]{1,0:T(8,128)(2,1)S(1)}, bf16[8192,128]{1,0:T(8,128)(2,1)}) fusion(), kind=kLoop, calls=%fused_computation.36 | loop fusion | flops 19922944 | bytes 4194304 | tf_op jit(solution)/shard_map/convert.13
  24.5 12.7 %fusion.28 = f32[1280,256]{0,1:T(8,128)} fusion(bf16[1280,8192]{1,0:T(8,128)(2,1)} %bitcast.100, bf16[8192,128]{1,0:T(8,128)(2,1)S(1)} %get-tuple-element.17, bf16[8192,128]{1,0:T(8,128)(2,1)} %get-tuple-element.18), kind=kOutput, calls=%fused_computation.42 | convolution fusion | flops 5377097728 | bytes 26476544 | tf_op jit(solution)/shard_map/dot_general | solution.py:104
  37.2 1.7 copy.7
  38.9 0.7 reshape.80
  39.6 1.5 fusion.125
  41.1 2.2 fusion.39
  43.2 2.2 fusion.40
  45.4 2.2 add_bitcast_fusion
  47.6 2.2 subtract_bitcast_fusion
  49.8 2.3 pad_maximum_fusion
  52.1 0.0 copy-start.1
  52.1 0.0 all-reduce.2.cloned.1.call-update
  52.1 0.0 all-gather.2.cloned.1.call-start
  52.2 144.5 %all-reduce.2.cloned.1.call-done = f32[2,128,32,128]{3,1,2,0:T(8,128)} async-done(((f32[2,128,32,128]{3,1,2,0:T(8,128)}), f32[2,128,32,128]{3,1,2,0:T(8,128)}) %all-reduce.2.cloned.1.call-update) | async-done | bytes 4194320 | tf_op jit(solution)/shard_map/psum | solution.py:111
  196.7 1.0 dynamic-slice_bitcast_fusion
  197.7 0.0 copy-done.1
  197.7 0.7 fusion.31
  198.5 0.1 fusion.43
  198.6 0.1 fusion.44
  198.6 0.7 pad_maximum_fusion.2
  199.3 0.0 all-gather.2.cloned.1.call-update
  199.4 16.1 %multiply_convert_fusion.1 = bf16[128,8192]{1,0:T(8,128)(2,1)S(1)} fusion(f32[128]{0:T(128)S(1)} %get-tuple-element.19), kind=kLoop, calls=%fused_computation.33 | loop fusion | flops 16777216 | bytes 2097664 | tf_op jit(solution)/shard_map/convert
  215.5 16.7 %multiply_convert_fusion = bf16[128,8192]{1,0:T(8,128)(2,1)} fusion(f32[128]{0:T(128)S(1)} %get-tuple-element.20), kind=kLoop, calls=%fused_computation.32 | loop fusion | flops 16777216 | bytes 2097664 | tf_op jit(solution)/shard_map/convert.1
  232.2 23.6 %all-gather.2.cloned.1.call-done = bf16[32,2,4,32,128]{4,2,0,3,1:T(4,128)(2,1)} async-done(((bf16[1,2,4,32,128]{4,2,0,3,1:T(4,128)(2,1)}), bf16[32,2,4,32,128]{4,2,0,3,1:T(4,128)(2,1)}) %all-gather.2.cloned.1.call-update) | async-done | bytes 2097168 | tf_op jit(solution)/shard_map/all_gather | solution.py:120
  255.8 2.4 fusion.124
  258.3 0.4 fusion.81
  258.7 0.4 fusion.85
  259.1 0.4 fusion.38
  259.6 0.4 fusion.37
  260.0 0.1 pad_maximum_fusion.1
  260.1 0.7 copy.10
  260.8 0.4 convert_element_type.48
  261.2 0.0 copy-start.2
  261.2 17.8 %fusion.19 = f32[40,32,8192]{2,1,0:T(8,128)} fusion(bf16[40,32,256]{2,1,0:T(8,128)(2,1)S(1)} %convert_element_type.48, bf16[128,8192]{1,0:T(8,128)(2,1)} %multiply_convert_fusion, bf16[128,8192]{1,0:T(8,128)(2,1)S(1)} %multiply_convert_fusion.1), kind=kOutput, calls=%fused_computation.29 | convolution fusion | flops 5377097728 | bytes 46792704 | tf_op jit(solution)/shard_map/dot_general | solution.py:125
  279.0 0.0 copy-done
  279.0 0.0 copy-done.2
  279.0 34.6 %fusion.7 = bf16[40,32,8192]{2,1,0:T(8,128)(2,1)} fusion(f32[40,32,8192]{2,1,0:T(8,128)} %fusion.19, f32[32]{0:T(128)S(1)} %copy-done.2, bf16[40,32,8192]{2,1,0:T(8,128)(2,1)} %param.4, bf16[32,32]{1,0:T(8,128)(2,1)S(1)} %copy-done), kind=kOutput, calls=%fused_computation.8 | convolution fusion | flops 786432000 | bytes 83888256 | tf_op jit(solution)/shard_map/oi,xiy->xoy/dot_general | solution.py:131
  (5 shorter events, 0.0 us)
Async XLA Ops:
  6.5 272.5 %copy-start = (bf16[32,32]{1,0:T(8,128)(2,1)S(1)}, bf16[32,32]{1,0:T(8,128)(2,1)}, u32[]{:S(2)}) copy-start(bf16[32,32]{1,0:T(8,128)(2,1)} %param.6) | copy-start | bytes 6148
  6.5 190.1 %all-reduce.2.cloned.1.call-start = ((), (), s32[]{:S(2)}) async-start(), calls=%async_computation | async-start | bytes 8388608 | tf_op jit(solution)/shard_map/psum | solution.py:111
  52.1 145.6 %copy-start.1 = (bf16[2,4,32,32,128]{4,3,2,1,0:T(8,128)(2,1)S(1)}, bf16[2,4,32,32,128]{4,3,2,1,0:T(8,128)(2,1)}, u32[]{:S(2)}) copy-start(bf16[2,4,32,32,128]{4,3,2,1,0:T(8,128)(2,1)} %param.5) | copy-start | bytes 6291460
  52.1 203.7 %all-gather.2.cloned.1.call-start = ((), (), s32[]{:S(2)}) async-start(), calls=%async_computation.1 | async-start | bytes 2162688 | tf_op jit(solution)/shard_map/all_gather | solution.py:120
  261.2 17.8 %copy-start.2 = (f32[32]{0:T(128)S(1)}, f32[32]{0:T(128)}, u32[]{:S(2)}) copy-start(f32[32]{0:T(128)} %param.7) | copy-start | bytes 388
Sparse Core Ops, SparseCore 0:
  52.2 144.4 all-reduce.1
  199.5 56.2 all-gather.1
where the time goes:
time: 321 us; the launch traced here: 320 us
  waiting for transfers between devices  168 us (52%)
  matrix products  75.5 us (24%)
  other arithmetic  54.8 us (17%)
  between operations  13.6 us (4%)
  local copies, waits for them, and re-layouts  8.4 us (3%)
    psum x1, waiting for transfers between devices, shards(): lax.psum(row_section(partial_value, cosine, sine), ('row', 'col'))  145 us
    another operation x3, other arithmetic  50.8 us
    dot_general x1, matrix products, shards(): jnp.einsum('oi,xiy->xoy', point_weight, field, preferred_element_type=jnp...  34.6 us
    all_gather x1, waiting for transfers between devices, shards(): gathered = lax.all_gather(mixed[None], ('row', 'col'), axis=0, tiled=True)  23.6 us
    dot_general x1, matrix products, shards(): jnp.dot(inverse_half.reshape(row_count * chan_count, 2 * modes_y), table_...  17.8 us
    dot_general x1, matrix products, shards(): jnp.dot(field.reshape(row_count * chan_count, col_count), table_y, prefer...  12.7 us
  transfers between devices with their start and end apart: 2, of which 2 were waited for; matrix products, arithmetic and copies ran while one was open for 10% of the time, Pallas kernels for 0%

commit v1 on v0

v1 whole, which is shorter than its diff:
```python
import functools
import math

import jax
import jax.numpy as jnp
import ml_dtypes
import numpy as np
from jax import lax
from jax.experimental import pallas as pl
from jax.experimental.pallas import tpu as pltpu
from jax.sharding import PartitionSpec as P

BF16 = ml_dtypes.bfloat16
MESH = pl.DeviceIdType.MESH
REMOTE = True


def phases(first, second, length):
    index = (first[:, None].astype(np.int64) * second[None, :]) % length
    return index.astype(np.float32) * np.float32(2.0 * math.pi / length)


def column_tables(modes_x, modes_y, length_y):
    freq = np.arange(modes_y)
    phase = phases(np.arange(length_y), freq, length_y)
    cosine, sine = np.cos(phase), np.sin(phase)
    scale = np.float32(1.0 / math.sqrt(length_y))
    forward = np.concatenate([cosine * scale, -sine * scale], axis=1).astype(BF16)
    factor = np.where(freq == 0, 1.0, 2.0).astype(np.float32) / np.float32(
        math.sqrt(2.0 * modes_x * modes_y)
    )
    inverse = np.concatenate([factor * cosine, -factor * sine], axis=1).T.astype(BF16)
    return forward, np.ascontiguousarray(inverse)


def row_tables(row_devices, block_x, row_count):
    modes_x, length_x = row_devices * block_x, row_devices * row_count
    index = np.arange(modes_x)
    freq = np.where(index < modes_x // 2, index, index - modes_x + length_x)
    phase = phases(freq, np.arange(length_x), length_x)
    shape = (row_devices, 1, block_x, row_devices, 1, row_count)
    cosine, sine = np.cos(phase).reshape(shape), np.sin(phase).reshape(shape)
    table = np.concatenate(
        [np.concatenate([cosine, sine], axis=4), np.concatenate([-sine, cosine], axis=4)], axis=1
    ).reshape(2 * modes_x, 2 * length_x)
    scaled = table * np.float32(1.0 / math.sqrt(length_x))
    high = scaled.astype(BF16)
    low = (scaled - high.astype(np.float32)).astype(BF16)
    return high, low, np.ascontiguousarray(table.T).astype(BF16)


def regroup(rows, channels):
    out = np.zeros((rows * channels, rows * channels), BF16)
    for row in range(rows):
        for channel in range(channels):
            out[channel * rows + row, row * channels + channel] = 1
    return out


CHUNK = 8


def forward_kernel(steps, field_ref, table_ref, perm_ref, out_ref, total, ordered):
    step = pl.program_id(0)
    rows, channels, width = field_ref.shape
    modes = out_ref.shape[2]

    @pl.when(step == 0)
    def _():
        total[...] = jnp.zeros_like(total)

    total[...] += jnp.dot(
        field_ref[...].reshape(rows * channels, width),
        table_ref[...],
        preferred_element_type=jnp.float32,
    )

    @pl.when(step == steps - 1)
    def _():
        size = CHUNK * channels
        for chunk in range(rows // CHUNK):
            part = total[chunk * size : (chunk + 1) * size, :]
            if out_ref.dtype == jnp.float32:
                moved = jnp.dot(
                    perm_ref[...].astype(jnp.float32),
                    part,
                    preferred_element_type=jnp.float32,
                    precision=lax.Precision.HIGHEST,
                )
            else:
                moved = jnp.dot(
                    perm_ref[...], part.astype(jnp.bfloat16), preferred_element_type=jnp.float32
                )
            moved = moved.reshape(channels, CHUNK, 2 * modes)
            at = chunk * CHUNK
            ordered[:, at : at + CHUNK, :] = moved[:, :, :modes]
            ordered[:, rows + at : rows + at + CHUNK, :] = moved[:, :, modes:]
        out_ref[...] = ordered[...].astype(out_ref.dtype)


def forward(field, table, out_type):
    rows, channels, cols = field.shape
    modes = table.shape[1] // 2
    width = min(cols, 1024)
    steps = cols // width
    perm = regroup(CHUNK, channels)
    return pl.pallas_call(
        functools.partial(forward_kernel, steps),
        out_shape=jax.ShapeDtypeStruct((channels, 2 * rows, modes), out_type),
        grid=(steps,),
        in_specs=[
            pl.BlockSpec((rows, channels, width), lambda y: (0, 0, y)),
            pl.BlockSpec((width, 2 * modes), lambda y: (y, 0)),
            pl.BlockSpec(perm.shape, lambda y: (0, 0)),
        ],
        out_specs=pl.BlockSpec((channels, 2 * rows, modes), lambda y: (0, 0, 0)),
        scratch_shapes=[
            pltpu.VMEM((rows * channels, 2 * modes), jnp.float32),
            pltpu.VMEM((channels, 2 * rows, modes), jnp.float32),
        ],
        compiler_params=pltpu.CompilerParams(vmem_limit_bytes=40 * 1024 * 1024),
        cost_estimate=pl.CostEstimate(
            flops=2 * rows * channels * cols * 2 * modes,
            bytes_accessed=2 * (rows * channels * cols + cols * 2 * modes),
            transcendentals=0,
        ),
    )(field, table, jnp.asarray(perm))


def inverse_kernel(field_ref, half_ref, table_ref, point_ref, bias_ref, out_ref):
    rows, channels, width = field_ref.shape
    size = CHUNK * channels
    tile = min(width, 256)

    @pl.loop(0, rows // CHUNK)
    def _(chunk):
        at = pl.multiple_of(chunk * CHUNK, CHUNK)
        half = half_ref[pl.ds(at, CHUNK)].reshape(size, half_ref.shape[2])
        for col in range(0, width, tile):
            values = field_ref[pl.ds(at, CHUNK), :, col : col + tile].reshape(size, tile)
            x = (
                jnp.dot(half, table_ref[:, col : col + tile], preferred_element_type=jnp.float32)
                + jnp.dot(point_ref[...], values, preferred_element_type=jnp.float32)
                + bias_ref[:, :tile]
            )
            inner = x * (math.sqrt(2.0 / math.pi) * 0.044715 * (x * x) + math.sqrt(2.0 / math.pi))
            scaled = 0.5 * x
            y = scaled * jnp.tanh(inner) + scaled
            out_ref[pl.ds(at, CHUNK), :, col : col + tile] = y.astype(out_ref.dtype).reshape(
                CHUNK, channels, tile
            )


def inverse(field, half, table, point_weight, bias):
    rows, channels, cols = field.shape
    depth = table.shape[0]
    width = min(cols, 1024)
    size = CHUNK * channels
    point = jnp.kron(jnp.eye(CHUNK, dtype=point_weight.dtype), point_weight)
    spread = jnp.broadcast_to(jnp.tile(bias, CHUNK)[:, None], (size, min(width, 256)))
    return pl.pallas_call(
        inverse_kernel,
        out_shape=jax.ShapeDtypeStruct(field.shape, jnp.bfloat16),
        grid=(cols // width,),
        in_specs=[
            pl.BlockSpec((rows, channels, width), lambda y: (0, 0, y)),
            pl.BlockSpec((rows, channels, depth), lambda y: (0, 0, 0)),
            pl.BlockSpec((depth, width), lambda y: (0, y)),
            pl.BlockSpec(point.shape, lambda y: (0, 0)),
            pl.BlockSpec(spread.shape, lambda y: (0, 0)),
        ],
        out_specs=pl.BlockSpec((rows, channels, width), lambda y: (0, 0, y)),
        compiler_params=pltpu.CompilerParams(vmem_limit_bytes=40 * 1024 * 1024),
        cost_estimate=pl.CostEstimate(
            flops=2 * rows * channels * cols * (depth + size),
            bytes_accessed=4 * rows * channels * cols,
            transcendentals=rows * channels * cols,
        ),
    )(field, half, table, point, spread)


def mix_modes(spectrum, spec_weight):
    weights = spec_weight.astype(jnp.float32)
    real, imag = spectrum[:, 0], spectrum[:, 1]
    product = functools.partial(jnp.einsum, "ijk,jiok->ojk", precision=lax.Precision.HIGHEST)
    out_real = product(real, weights[0]) - product(imag, weights[1])
    out_imag = product(real, weights[1]) + product(imag, weights[0])
    return jnp.stack([out_real, out_imag], axis=1).astype(jnp.bfloat16)


def swap(blocks):
    count, own, rows, modes = blocks.shape
    got = lax.all_to_all(blocks, "row", 0, 0, tiled=True)
    return got.transpose(1, 0, 2, 3).reshape(own, count * rows, modes)


def give(values, count):
    own, size, modes = values.shape
    blocks = values.reshape(own, count, size // count, modes).transpose(1, 0, 2, 3)
    got = lax.all_to_all(blocks, "row", 0, 0, tiled=True)
    return got.reshape(count * own, size // count, modes)


def middle(partial_value, spec_weight, tables):
    high, low, back = tables
    channels, rows, modes = partial_value.shape
    count = lax.axis_size("row")
    block_x = spec_weight.shape[1]
    part = swap(partial_value.reshape(count, channels // count, rows, modes))
    transform = functools.partial(
        jnp.einsum, "am,cmk->cak", preferred_element_type=jnp.float32
    )
    spectrum = give(transform(high, part) + transform(low, part), count)
    mixed = mix_modes(spectrum.reshape(channels, 2, block_x, modes), spec_weight)
    mixed = swap(mixed.reshape(count, channels // count, 2 * block_x, modes))
    half = jnp.einsum("ma,cak->cmk", back, mixed, preferred_element_type=jnp.float32)
    return give(half.astype(jnp.bfloat16), count)


def middle_kernel(
    n, part_ref, high_hbm, low_hbm, back_hbm, weight_hbm, out_ref,
    high, low, back, weight, part_in, spec_out, spec_in, mix_out, mix_in, half_out,
    load_sem, send_sem, recv_sem,
):
    me = lax.axis_index("row")
    block_x, channels = weight.shape[1], weight.shape[3]
    modes = weight.shape[4]
    pairs = [(high_hbm, high), (low_hbm, low), (weight_hbm, weight), (back_hbm, back)]
    loads = [
        pltpu.make_async_copy(src, dst, load_sem.at[at]) for at, (src, dst) in enumerate(pairs)
    ]
    for load in loads:
        load.start()

    barrier = pltpu.get_barrier_semaphore()

    @pl.loop(1, n)
    def _(shift):
        pl.semaphore_signal(
            barrier, inc=1, device_id={"row": lax.rem(me + shift, n)}, device_id_type=MESH
        )

    pl.semaphore_wait(barrier, n - 1)

    def copy(phase, src, dst, shift):
        to = lax.rem(me + shift, n)
        return pltpu.make_async_remote_copy(
            src_ref=src.at[to],
            dst_ref=dst.at[me],
            send_sem=send_sem.at[phase, shift],
            recv_sem=recv_sem.at[phase, shift],
            device_id={"row": to},
            device_id_type=MESH,
        )

    def exchange(phase, src, dst):
        @pl.loop(1, n)
        def _(shift):
            copy(phase, src, dst, shift).start()

        dst[me] = src[me]

        @pl.loop(1, n)
        def _(shift):
            copy(phase, src, dst, shift).wait_recv()

    exchange(0, part_ref, part_in)
    loads[0].wait()
    loads[1].wait()
    part = part_in[...].reshape(n * part_in.shape[1], modes)
    spectrum = jnp.dot(high[...], part, preferred_element_type=jnp.float32) + jnp.dot(
        low[...], part, preferred_element_type=jnp.float32
    )
    spec_out[...] = spectrum.reshape(spec_out.shape)
    exchange(1, spec_out, spec_in)
    loads[2].wait()
    for mode in range(block_x):

        def add(at, sums, mode=mode):
            real, imag = sums
            a = spec_in[at, mode : mode + 1, :]
            b = spec_in[at, block_x + mode : block_x + mode + 1, :]
            c = weight[0, mode, at].astype(jnp.float32)
            d = weight[1, mode, at].astype(jnp.float32)
            return real + (a * c - b * d), imag + (a * d + b * c)

        zero = jnp.zeros((channels, modes), jnp.float32)
        real, imag = lax.fori_loop(0, channels, add, (zero, zero))
        mix_out[:, mode, :] = real
        mix_out[:, block_x + mode, :] = imag
    exchange(2, mix_out, mix_in)
    loads[3].wait()
    mixed = mix_in[...].reshape(n * 2 * block_x, modes).astype(jnp.bfloat16)
    half = jnp.dot(back[...], mixed, preferred_element_type=jnp.float32)
    half_out[...] = half.astype(jnp.bfloat16).reshape(half_out.shape)
    exchange(3, half_out, out_ref)
    for phase, (src, dst) in enumerate(
        [(part_ref, part_in), (spec_out, spec_in), (mix_out, mix_in), (half_out, out_ref)]
    ):

        @pl.loop(1, n)
        def _(shift, phase=phase, src=src, dst=dst):
            copy(phase, src, dst, shift).wait_send()


def remote_middle(partial_value, spec_weight, tables):
    count = lax.axis_size("row")
    channels, rows, modes = partial_value.shape
    block_x = spec_weight.shape[1]
    vmem = pl.BlockSpec(memory_space=pltpu.VMEM)
    wide = pltpu.VMEM(partial_value.shape, jnp.bfloat16)
    narrow = pltpu.VMEM((channels, 2 * block_x, modes), jnp.float32)
    return pl.pallas_call(
        functools.partial(middle_kernel, count),
        out_shape=jax.ShapeDtypeStruct(partial_value.shape, jnp.bfloat16),
        in_specs=[vmem] + [pl.BlockSpec(memory_space=pl.ANY)] * 4,
        out_specs=vmem,
        scratch_shapes=[pltpu.VMEM(table.shape, jnp.bfloat16) for table in tables]
        + [pltpu.VMEM(spec_weight.shape, jnp.bfloat16)]
        + [wide, narrow, narrow, narrow, narrow, wide]
        + [
            pltpu.SemaphoreType.DMA((4,)),
            pltpu.SemaphoreType.DMA((4, count)),
            pltpu.SemaphoreType.DMA((4, count)),
        ],
        compiler_params=pltpu.CompilerParams(
            collective_id=0, has_side_effects=True, vmem_limit_bytes=32 * 1024 * 1024
        ),
    )(partial_value, *tables, spec_weight)


def shards(field, spec_weight, point_weight, bias):
    row_count, chan_count, col_count = field.shape
    row_devices = lax.axis_size("row")
    col_devices = lax.axis_size("col")
    block_x = spec_weight.shape[1]
    modes_y = spec_weight.shape[4] * col_devices
    modes_x = block_x * row_devices
    table_y, table_back = column_tables(modes_x, modes_y, col_count * col_devices)
    table_y, table_back = jnp.asarray(table_y), jnp.asarray(table_back)
    tables = [jnp.asarray(table) for table in row_tables(row_devices, block_x, row_count)]
    if col_devices > 1:
        start = lax.axis_index("col") * col_count
        table_y = lax.dynamic_slice_in_dim(table_y, start, col_count, 0)
        table_back = lax.dynamic_slice_in_dim(table_back, start, col_count, 1)
        whole = forward(field, table_y, jnp.float32)
        own = lax.psum_scatter(whole, "col", scatter_dimension=2, tiled=True)
        half = middle(own.astype(jnp.bfloat16), spec_weight, tables)
        half = lax.all_gather(half, "col", axis=2, tiled=True)
    else:
        partial_value = forward(field, table_y, jnp.bfloat16)
        if REMOTE and chan_count == row_devices:
            half = remote_middle(partial_value, spec_weight, tables)
        else:
            half = middle(partial_value, spec_weight, tables)
    half = half.reshape(chan_count, 2, row_count, modes_y).transpose(2, 0, 1, 3)
    half = half.reshape(row_count, chan_count, 2 * modes_y)
    return inverse(field, half, table_back, point_weight, bias)


def solution(mesh):
    placed = (P(("group", "row"), None, "col"), P(None, "row", None, None, "col"), P(), P())
    return jax.shard_map(
        shards,
        mesh=mesh,
        in_specs=placed,
        out_specs=P(("group", "row"), None, "col"),
        check_vma=False,
    )
```

time: 321 us -> 104 us (0.32)
  the two profiles are of different devices: /device:TPU:0 before, /device:TPU:13 now
where the time goes in v1:
time: 104 us; the launch traced here: 103 us
  Pallas kernels  94.8 us (91%)
  local copies, waits for them, and re-layouts  7.59 us (7%)
    pallas_call x1, Pallas kernels, remote_middle(): pl.pallas_call(functools.partial(middle_kernel, count), out_shape=jax.Sha...  55.5 us
    pallas_call x1, Pallas kernels, inverse(): pl.pallas_call(inverse_kernel, out_shape=jax.ShapeDtypeStruct(field.shape...  26.5 us
    pallas_call x1, Pallas kernels, forward(): pl.pallas_call(functools.partial(forward_kernel, steps), out_shape=jax.Sh...  12.8 us
    unnamed x14, local copies, waits for them, and re-layouts  5.29 us

profile of v1, /device:TPU:13, one launch (start us, length us, event | category | flops | bytes accessed | tf_op | source)
XLA Modules:
  0.0 103.3 jit_solution(5182441056784080643)
XLA Ops:
  0.0 0.7 tile.2
  0.7 0.1 broadcast_in_dim.11
  0.7 0.1 broadcast_in_dim.12.bias_ref
  0.8 0.8 broadcast_multiply_fusion
  1.7 0.4 mul.27.point_ref
  2.0 0.0 copy-start.1
  2.0 2.2 %copy-done.1 = bf16[8192,256]{1,0:T(8,128)(2,1)S(1)} copy-done((bf16[8192,256]{1,0:T(8,128)(2,1)S(1)}, bf16[8192,256]{1,0:T(8,128)(2,1)}, u32[]{:S(2)}) %copy-start.1) | copy-done | bytes 4194328
  4.2 0.0 copy-start.6
  4.2 0.9 copy-done.6
  5.1 0.0 copy-start.2
  5.1 0.0 copy-start.3
  5.1 0.0 copy-start.4
  5.1 0.0 copy-start.5
  5.1 12.8 %shard_map.100.part_ref = bf16[32,80,128]{2,1,0:T(8,128)(2,1)S(1)} custom-call(bf16[40,32,8192]{2,1,0:T(8,128)(2,1)} %field_ref.3, bf16[8192,256]{1,0:T(8,128)(2,1)S(1)} %copy-done.1, bf16[256,256]{1,0:T(8,128)(2,1)S(1)} %copy-done.6), custom_call_target="tpu_custom_call" | custom-call | flops 5368709120 | bytes 25165824 | tf_op jit(solution)/shard_map/pallas_call | solution.py:107
  17.9 0.0 copy-done.2
  17.9 0.0 copy-done.3
  17.9 0.0 copy-done.4
  17.9 0.0 copy-done.5
  17.9 55.5 %shard_map.101 = bf16[32,80,128]{2,1,0:T(8,128)(2,1)S(1)} custom-call(bf16[32,80,128]{2,1,0:T(8,128)(2,1)S(1)} %shard_map.100.part_ref, bf16[256,2560]{1,0:T(8,128)(2,1)S(1)} %copy-done.5, bf16[256,2560]{1,0:T(8,128)(2,1)S(1)} %copy-done.4, bf16[2560,256]{1,0:T(8,128)(2,1)S(1)} %copy-done.3, bf16[2,4,32,32,128]{4,3,2,1,0:T(8,128)(2,1)S(1)} %copy-done.2), custom_call_target="tpu_custom_call" | custom-call | tf_op jit(solution)/shard_map/pallas_call | solution.py:313
  73.4 0.7 copy.13
  74.1 0.4 reshape.23.half_ref
  74.6 0.0 copy-start
  74.6 2.2 %copy-done = bf16[256,8192]{1,0:T(8,128)(2,1)S(1)} copy-done((bf16[256,8192]{1,0:T(8,128)(2,1)S(1)}, bf16[256,8192]{1,0:T(8,128)(2,1)}, u32[]{:S(2)}) %copy-start) | copy-done | bytes 4194328
  76.8 26.5 %shard_map.102 = bf16[40,32,8192]{2,1,0:T(8,128)(2,1)} custom-call(bf16[40,32,8192]{2,1,0:T(8,128)(2,1)} %field_ref.3, bf16[40,32,256]{2,1,0:T(8,128)(2,1)S(1)} %reshape.23.half_ref, bf16[256,8192]{1,0:T(8,128)(2,1)S(1)} %copy-done, bf16[256,256]{1,0:T(8,128)(2,1)S(1)} %mul.27.point_ref, f32[256,256]{1,0:T(8,128)S(1)} %broadcast_in_dim.12.bias_ref), custom_call_target="tpu_custom_call" | custom-call | flops 10737418240 | bytes 41943040 | tf_op jit(solution)/shard_map/pallas_call | solution.py:161
  (1 shorter events, 0.0 us)
Async XLA Ops:
  2.0 2.2 %copy-start.1 = (bf16[8192,256]{1,0:T(8,128)(2,1)S(1)}, bf16[8192,256]{1,0:T(8,128)(2,1)}, u32[]{:S(2)}) copy-start(bf16[8192,256]{1,0:T(8,128)(2,1)} %constant.12.clone.table_ref) | copy-start | bytes 12582916
  4.2 0.9 copy-start.6
  5.1 12.8 %copy-start.2 = (bf16[2,4,32,32,128]{4,3,2,1,0:T(8,128)(2,1)S(1)}, bf16[2,4,32,32,128]{4,3,2,1,0:T(8,128)(2,1)}, u32[]{:S(2)}) copy-start(bf16[2,4,32,32,128]{4,3,2,1,0:T(8,128)(2,1)} %weight_hbm.1) | copy-start | bytes 6291460
  5.1 12.8 %copy-start.3 = (bf16[2560,256]{1,0:T(8,128)(2,1)S(1)}, bf16[2560,256]{1,0:T(8,128)(2,1)}, u32[]{:S(2)}) copy-start(bf16[2560,256]{1,0:T(8,128)(2,1)} %constant.16.clone.back_hbm) | copy-start | bytes 3932164
  5.1 12.8 %copy-start.4 = (bf16[256,2560]{1,0:T(8,128)(2,1)S(1)}, bf16[256,2560]{1,0:T(8,128)(2,1)}, u32[]{:S(2)}) copy-start(bf16[256,2560]{1,0:T(8,128)(2,1)} %constant.15.clone.low_hbm) | copy-start | bytes 3932164
  5.1 12.8 %copy-start.5 = (bf16[256,2560]{1,0:T(8,128)(2,1)S(1)}, bf16[256,2560]{1,0:T(8,128)(2,1)}, u32[]{:S(2)}) copy-start(bf16[256,2560]{1,0:T(8,128)(2,1)} %constant.14.clone.high_hbm) | copy-start | bytes 3932164
  74.6 2.2 %copy-start = (bf16[256,8192]{1,0:T(8,128)(2,1)S(1)}, bf16[256,8192]{1,0:T(8,128)(2,1)}, u32[]{:S(2)}) copy-start(bf16[256,8192]{1,0:T(8,128)(2,1)} %constant.13.clone.table_ref) | copy-start | bytes 12582916

commit v2 on v1

--- a/solution.py
+++ b/solution.py
@@ -12,7 +12,6 @@
 
 BF16 = ml_dtypes.bfloat16
 MESH = pl.DeviceIdType.MESH
-REMOTE = True
 
 
 def phases(first, second, length):
@@ -30,7 +29,8 @@
         math.sqrt(2.0 * modes_x * modes_y)
     )
     inverse = np.concatenate([factor * cosine, -factor * sine], axis=1).T.astype(BF16)
-    return forward, np.ascontiguousarray(inverse)
+    halved = (0.5 * inverse.astype(np.float32)).astype(BF16)
+    return forward, np.ascontiguousarray(halved)
 
 
 def row_tables(row_devices, block_x, row_count):
@@ -101,7 +101,7 @@
 def forward(field, table, out_type):
     rows, channels, cols = field.shape
     modes = table.shape[1] // 2
-    width = min(cols, 1024)
+    width = min(cols, 2048)
     steps = cols // width
     perm = regroup(CHUNK, channels)
     return pl.pallas_call(
@@ -118,7 +118,7 @@
             pltpu.VMEM((rows * channels, 2 * modes), jnp.float32),
             pltpu.VMEM((channels, 2 * rows, modes), jnp.float32),
         ],
-        compiler_params=pltpu.CompilerParams(vmem_limit_bytes=40 * 1024 * 1024),
+        compiler_params=pltpu.CompilerParams(vmem_limit_bytes=60 * 1024 * 1024),
         cost_estimate=pl.CostEstimate(
             flops=2 * rows * channels * cols * 2 * modes,
             bytes_accessed=2 * (rows * channels * cols + cols * 2 * modes),
@@ -143,21 +143,18 @@
                 + jnp.dot(point_ref[...], values, preferred_element_type=jnp.float32)
                 + bias_ref[:, :tile]
             )
-            inner = x * (math.sqrt(2.0 / math.pi) * 0.044715 * (x * x) + math.sqrt(2.0 / math.pi))
-            scaled = 0.5 * x
-            y = scaled * jnp.tanh(inner) + scaled
+            rate = 2.0 * math.sqrt(2.0 / math.pi)
+            y = x * jnp.tanh(x * (rate * 4.0 * 0.044715 * (x * x) + rate)) + x
             out_ref[pl.ds(at, CHUNK), :, col : col + tile] = y.astype(out_ref.dtype).reshape(
                 CHUNK, channels, tile
             )
 
 
-def inverse(field, half, table, point_weight, bias):
+def inverse(field, half, table, point, spread):
     rows, channels, cols = field.shape
     depth = table.shape[0]
-    width = min(cols, 1024)
+    width = min(cols, 2048)
     size = CHUNK * channels
-    point = jnp.kron(jnp.eye(CHUNK, dtype=point_weight.dtype), point_weight)
-    spread = jnp.broadcast_to(jnp.tile(bias, CHUNK)[:, None], (size, min(width, 256)))
     return pl.pallas_call(
         inverse_kernel,
         out_shape=jax.ShapeDtypeStruct(field.shape, jnp.bfloat16),
@@ -170,7 +167,7 @@
             pl.BlockSpec(spread.shape, lambda y: (0, 0)),
         ],
         out_specs=pl.BlockSpec((rows, channels, width), lambda y: (0, 0, y)),
-        compiler_params=pltpu.CompilerParams(vmem_limit_bytes=40 * 1024 * 1024),
+        compiler_params=pltpu.CompilerParams(vmem_limit_bytes=60 * 1024 * 1024),
         cost_estimate=pl.CostEstimate(
             flops=2 * rows * channels * cols * (depth + size),
             bytes_accessed=4 * rows * channels * cols,
@@ -217,116 +214,220 @@
     return give(half.astype(jnp.bfloat16), count)
 
 
+PLANE = 8
+
+
 def middle_kernel(
-    n, part_ref, high_hbm, low_hbm, back_hbm, weight_hbm, out_ref,
-    high, low, back, weight, part_in, spec_out, spec_in, mix_out, mix_in, half_out,
-    load_sem, send_sem, recv_sem,
+    outer, part_ref, point_ref, bias_ref, high_hbm, low_hbm, back_hbm, weight_hbm,
+    out_ref, point_out, bias_out,
+    high, low, back, weight, part_in, sums, partial_out, partial_in, spec_out, spec_in,
+    mix_out, mix_in, modes_in, half_out, load_sem, send_sem, recv_sem,
 ):
     me = lax.axis_index("row")
-    block_x, channels = weight.shape[1], weight.shape[3]
-    modes = weight.shape[4]
-    pairs = [(high_hbm, high), (low_hbm, low), (weight_hbm, weight), (back_hbm, back)]
+    level, place = me // PLANE, lax.rem(me, PLANE)
+    block_x, channels, modes = weight.shape[1], weight.shape[3], weight.shape[4]
+    own = channels // PLANE
+    span = high.shape[1]
+    start = pl.multiple_of(level * span, span)
+    pairs = [
+        (high_hbm.at[:, pl.ds(start, span)], high),
+        (low_hbm.at[:, pl.ds(start, span)], low),
+        (weight_hbm, weight),
+        (back_hbm.at[pl.ds(start, span), :], back),
+    ]
     loads = [
         pltpu.make_async_copy(src, dst, load_sem.at[at]) for at, (src, dst) in enumerate(pairs)
     ]
     for load in loads:
         load.start()
 
+    def in_plane(shift):
+        return lax.rem(place + shift, PLANE)
+
+    def in_line(shift):
+        return lax.rem(level + shift, outer)
+
     barrier = pltpu.get_barrier_semaphore()
 
-    @pl.loop(1, n)
+    @pl.loop(1, PLANE)
     def _(shift):
-        pl.semaphore_signal(
-            barrier, inc=1, device_id={"row": lax.rem(me + shift, n)}, device_id_type=MESH
-        )
-
-    pl.semaphore_wait(barrier, n - 1)
-
-    def copy(phase, src, dst, shift):
-        to = lax.rem(me + shift, n)
+        to = level * PLANE + in_plane(shift)
+        pl.semaphore_signal(barrier, inc=1, device_id={"row": to}, device_id_type=MESH)
+
+    @pl.loop(1, outer)
+    def _(shift):
+        to = in_line(shift) * PLANE + place
+        pl.semaphore_signal(barrier, inc=1, device_id={"row": to}, device_id_type=MESH)
+
+    size = bias_out.shape[0]
+    shape = (size, channels)
+    pick = lax.broadcasted_iota(jnp.int32, shape, 0) % channels == lax.broadcasted_iota(
+        jnp.int32, shape, 1
+    )
+    pick = pick.astype(jnp.float32)
+    along = (((1,), (1,)), ((), ()))
+    tall = jnp.dot(pick.astype(jnp.bfloat16), point_ref[...], preferred_element_type=jnp.float32)
+    full = lax.dot_general(
+        tall.astype(jnp.bfloat16),
+        pick.astype(jnp.bfloat16),
+        along,
+        preferred_element_type=jnp.float32,
+    )
+    shape = (size, size)
+    same = lax.broadcasted_iota(jnp.int32, shape, 0) // channels == lax.broadcasted_iota(
+        jnp.int32, shape, 1
+    ) // channels
+    point_out[...] = jnp.where(same, 0.5 * full, 0.0).astype(jnp.bfloat16)
+    bias_out[...] = 0.5 * lax.dot_general(
+        pick,
+        jnp.broadcast_to(bias_ref[...], (size, channels)),
+        along,
+        preferred_element_type=jnp.float32,
+        precision=lax.Precision.HIGHEST,
+    )
+    pl.semaphore_wait(barrier, PLANE - 1 + outer - 1)
+
+    def copy(src, dst, phase, piece, shift, to):
         return pltpu.make_async_remote_copy(
-            src_ref=src.at[to],
-            dst_ref=dst.at[me],
-            send_sem=send_sem.at[phase, shift],
-            recv_sem=recv_sem.at[phase, shift],
+            src_ref=src,
+            dst_ref=dst,
+            send_sem=send_sem.at[phase, piece, shift],
+            recv_sem=recv_sem.at[phase, piece, shift],
             device_id={"row": to},
             device_id_type=MESH,
         )
 
-    def exchange(phase, src, dst):
-        @pl.loop(1, n)
+    def plane_copy(phase, piece, shift):
+        to = in_plane(shift)
+        src, dst = [
+            lambda: (part_ref.at[to * own + piece], part_in.at[piece, place]),
+            lambda: (spec_out.at[to], spec_in.at[place]),
+            lambda: (mix_out.at[to], mix_in.at[place]),
+            lambda: (half_out.at[piece, to], out_ref.at[place * own + piece]),
+        ][phase]()
+        return copy(src, dst, phase, piece, shift, level * PLANE + to)
+
+    def line_copy(phase, piece, shift):
+        to = in_line(shift)
+        src, dst = [
+            lambda: (partial_out.at[piece, to], partial_in.at[piece, shift]),
+            lambda: (modes_in.at[piece, level], modes_in.at[piece, level]),
+        ][phase]()
+        return copy(src, dst, 4 + phase, piece, shift, to * PLANE + place)
+
+    def each(make, phase, piece, count, act):
+        @pl.loop(1, count)
         def _(shift):
-            copy(phase, src, dst, shift).start()
-
-        dst[me] = src[me]
-
-        @pl.loop(1, n)
-        def _(shift):
-            copy(phase, src, dst, shift).wait_recv()
-
-    exchange(0, part_ref, part_in)
+            getattr(make(phase, piece, shift), act)()
+
+    for piece in range(own):
+        each(plane_copy, 0, piece, PLANE, "start")
+    for piece in range(own):
+        part_in[piece, place] = part_ref[place * own + piece]
     loads[0].wait()
     loads[1].wait()
-    part = part_in[...].reshape(n * part_in.shape[1], modes)
-    spectrum = jnp.dot(high[...], part, preferred_element_type=jnp.float32) + jnp.dot(
-        low[...], part, preferred_element_type=jnp.float32
-    )
-    spec_out[...] = spectrum.reshape(spec_out.shape)
-    exchange(1, spec_out, spec_in)
+    for piece in range(own):
+        each(plane_copy, 0, piece, PLANE, "wait_recv")
+        part = part_in[piece].reshape(span, modes)
+        spectrum = jnp.dot(high[...], part, preferred_element_type=jnp.float32) + jnp.dot(
+            low[...], part, preferred_element_type=jnp.float32
+        )
+        spectrum = spectrum.reshape(sums.shape[1:])
+        sums[piece] = spectrum
+        partial_out[piece] = spectrum.astype(jnp.bfloat16)
+        each(line_copy, 0, piece, outer, "start")
+    for piece in range(own):
+        each(line_copy, 0, piece, outer, "wait_recv")
+        total = sums[piece, level]
+        for shift in range(1, outer):
+            total += partial_in[piece, shift].astype(jnp.float32)
+        spec_out[:, piece] = total.reshape(PLANE, 2 * block_x, modes)
+    each(plane_copy, 1, 0, PLANE, "start")
+    spec_in[place] = spec_out[place]
     loads[2].wait()
+    each(plane_copy, 1, 0, PLANE, "wait_recv")
     for mode in range(block_x):
 
-        def add(at, sums, mode=mode):
-            real, imag = sums
-            a = spec_in[at, mode : mode + 1, :]
-            b = spec_in[at, block_x + mode : block_x + mode + 1, :]
-            c = weight[0, mode, at].astype(jnp.float32)
-            d = weight[1, mode, at].astype(jnp.float32)
-            return real + (a * c - b * d), imag + (a * d + b * c)
+        def add(at, carry, mode=mode):
+            real, imag = carry
+            for piece in range(own):
+                a = spec_in[at, piece, mode : mode + 1, :]
+                b = spec_in[at, piece, block_x + mode : block_x + mode + 1, :]
+                c = weight[0, mode, at * own + piece].astype(jnp.float32)
+                d = weight[1, mode, at * own + piece].astype(jnp.float32)
+                real, imag = real + (a * c - b * d), imag + (a * d + b * c)
+            return real, imag
 
         zero = jnp.zeros((channels, modes), jnp.float32)
-        real, imag = lax.fori_loop(0, channels, add, (zero, zero))
-        mix_out[:, mode, :] = real
-        mix_out[:, block_x + mode, :] = imag
-    exchange(2, mix_out, mix_in)
+        real, imag = lax.fori_loop(0, PLANE, add, (zero, zero))
+        mix_out[:, :, mode, :] = real.reshape(PLANE, own, modes)
+        mix_out[:, :, block_x + mode, :] = imag.reshape(PLANE, own, modes)
+    each(plane_copy, 2, 0, PLANE, "start")
+    mix_in[place] = mix_out[place]
+    each(plane_copy, 2, 0, PLANE, "wait_recv")
+    for piece in range(own):
+        mixed = mix_in[:, piece].reshape(PLANE * 2 * block_x, modes)
+        modes_in[piece, level] = mixed.astype(jnp.bfloat16)
+        each(line_copy, 1, piece, outer, "start")
     loads[3].wait()
-    mixed = mix_in[...].reshape(n * 2 * block_x, modes).astype(jnp.bfloat16)
-    half = jnp.dot(back[...], mixed, preferred_element_type=jnp.float32)
-    half_out[...] = half.astype(jnp.bfloat16).reshape(half_out.shape)
-    exchange(3, half_out, out_ref)
-    for phase, (src, dst) in enumerate(
-        [(part_ref, part_in), (spec_out, spec_in), (mix_out, mix_in), (half_out, out_ref)]
-    ):
-
-        @pl.loop(1, n)
-        def _(shift, phase=phase, src=src, dst=dst):
-            copy(phase, src, dst, shift).wait_send()
-
-
-def remote_middle(partial_value, spec_weight, tables):
-    count = lax.axis_size("row")
+    for piece in range(own):
+        each(line_copy, 1, piece, outer, "wait_recv")
+        mixed = modes_in[piece].reshape(back.shape[1], modes)
+        half = jnp.dot(back[...], mixed, preferred_element_type=jnp.float32)
+        half_out[piece] = half.astype(jnp.bfloat16).reshape(half_out.shape[1:])
+        each(plane_copy, 3, piece, PLANE, "start")
+        out_ref[place * own + piece] = half_out[piece, place]
+    for piece in range(own):
+        each(plane_copy, 3, piece, PLANE, "wait_recv")
+    for phase in range(4):
+        for piece in range(own if phase in (0, 3) else 1):
+            each(plane_copy, phase, piece, PLANE, "wait_send")
+    for phase in range(2):
+        for piece in range(own):
+            each(line_copy, phase, piece, outer, "wait_send")
+
+
+def remote_middle(partial_value, spec_weight, point_weight, bias, tables):
+    outer = lax.axis_size("row") // PLANE
     channels, rows, modes = partial_value.shape
     block_x = spec_weight.shape[1]
+    own = channels // PLANE
+    span, depth = PLANE * rows, 2 * block_x
+    size = CHUNK * channels
     vmem = pl.BlockSpec(memory_space=pltpu.VMEM)
-    wide = pltpu.VMEM(partial_value.shape, jnp.bfloat16)
-    narrow = pltpu.VMEM((channels, 2 * block_x, modes), jnp.float32)
+    half, full = jnp.bfloat16, jnp.float32
     return pl.pallas_call(
-        functools.partial(middle_kernel, count),
-        out_shape=jax.ShapeDtypeStruct(partial_value.shape, jnp.bfloat16),
-        in_specs=[vmem] + [pl.BlockSpec(memory_space=pl.ANY)] * 4,
-        out_specs=vmem,
-        scratch_shapes=[pltpu.VMEM(table.shape, jnp.bfloat16) for table in tables]
-        + [pltpu.VMEM(spec_weight.shape, jnp.bfloat16)]
-        + [wide, narrow, narrow, narrow, narrow, wide]
-        + [
+        functools.partial(middle_kernel, outer),
+        out_shape=[
+            jax.ShapeDtypeStruct(partial_value.shape, half),
+            jax.ShapeDtypeStruct((size, size), half),
+            jax.ShapeDtypeStruct((size, size), full),
+        ],
+        in_specs=[vmem] * 3 + [pl.BlockSpec(memory_space=pl.ANY)] * 4,
+        out_specs=[vmem] * 3,
+        scratch_shapes=[
+            pltpu.VMEM((outer * PLANE * depth, span), half),
+            pltpu.VMEM((outer * PLANE * depth, span), half),
+            pltpu.VMEM((span, outer * PLANE * depth), half),
+            pltpu.VMEM(spec_weight.shape, half),
+            pltpu.VMEM((own, PLANE, rows, modes), half),
+            pltpu.VMEM((own, outer, PLANE * depth, modes), full),
+            pltpu.VMEM((own, outer, PLANE * depth, modes), half),
+            pltpu.VMEM((own, outer, PLANE * depth, modes), half),
+            pltpu.VMEM((PLANE, own, depth, modes), full),
+            pltpu.VMEM((PLANE, own, depth, modes), full),
+            pltpu.VMEM((PLANE, own, depth, modes), full),
+            pltpu.VMEM((PLANE, own, depth, modes), full),
+            pltpu.VMEM((own, outer, PLANE * depth, modes), half),
+            pltpu.VMEM((own, PLANE, rows, modes), half),
             pltpu.SemaphoreType.DMA((4,)),
-            pltpu.SemaphoreType.DMA((4, count)),
-            pltpu.SemaphoreType.DMA((4, count)),
+            pltpu.SemaphoreType.DMA((6, own, PLANE)),
+            pltpu.SemaphoreType.DMA((6, own, PLANE)),
         ],
         compiler_params=pltpu.CompilerParams(
             collective_id=0, has_side_effects=True, vmem_limit_bytes=32 * 1024 * 1024
         ),
-    )(partial_value, *tables, spec_weight)
+    )(partial_value, point_weight, bias[None, :], *tables, spec_weight)
 
 
 def shards(field, spec_weight, point_weight, bias):
@@ -339,6 +440,12 @@
     table_y, table_back = column_tables(modes_x, modes_y, col_count * col_devices)
     table_y, table_back = jnp.asarray(table_y), jnp.asarray(table_back)
     tables = [jnp.asarray(table) for table in row_tables(row_devices, block_x, row_count)]
+    direct = col_devices == 1 and row_devices % PLANE == 0 and chan_count % PLANE == 0
+    direct = direct and (2 * block_x) % 8 == 0 and row_count % 8 == 0
+    if not direct:
+        size = CHUNK * chan_count
+        point = 0.5 * jnp.kron(jnp.eye(CHUNK, dtype=point_weight.dtype), point_weight)
+        spread = 0.5 * jnp.broadcast_to(jnp.tile(bias, CHUNK)[:, None], (size, size))
     if col_devices > 1:
         start = lax.axis_index("col") * col_count
         table_y = lax.dynamic_slice_in_dim(table_y, start, col_count, 0)
@@ -349,13 +456,15 @@
         half = lax.all_gather(half, "col", axis=2, tiled=True)
     else:
         partial_value = forward(field, table_y, jnp.bfloat16)
-        if REMOTE and chan_count == row_devices:
-            half = remote_middle(partial_value, spec_weight, tables)
+        if direct:
+            half, point, spread = remote_middle(
+                partial_value, spec_weight, point_weight, bias, tables
+            )
         else:
             half = middle(partial_value, spec_weight, tables)
     half = half.reshape(chan_count, 2, row_count, modes_y).transpose(2, 0, 1, 3)
     half = half.reshape(row_count, chan_count, 2 * modes_y)
-    return inverse(field, half, table_back, point_weight, bias)
+    return inverse(field, half, table_back, point, spread)
 
 
 def solution(mesh):

time: 104 us -> 87.7 us (0.84)
  the two profiles are of different devices: /device:TPU:13 before, /device:TPU:0 now
where the time goes in v2:
time: 87.7 us; the launch traced here: 87.4 us
  Pallas kernels  81.7 us (93%)
  local copies, waits for them, and re-layouts  5.69 us (6%)
    pallas_call x1, Pallas kernels, remote_middle(): pl.pallas_call(functools.partial(middle_kernel, outer), out_shape=[jax.Sh...  43.4 us
    pallas_call x1, Pallas kernels, inverse(): pl.pallas_call(inverse_kernel, out_shape=jax.ShapeDtypeStruct(field.shape...  24.7 us
    pallas_call x1, Pallas kernels, forward(): pl.pallas_call(functools.partial(forward_kernel, steps), out_shape=jax.Sh...  13.6 us
    unnamed x18, local copies, waits for them, and re-layouts  3.74 us

profile of v2, /device:TPU:0, one launch (start us, length us, event | category | flops | bytes accessed | tf_op | source)
XLA Modules:
  0.0 87.4 jit_solution(3013116791548032773)
XLA Ops:
  0.0 0.0 copy-start.1
  0.0 0.0 copy-start.2
  0.0 0.0 copy-start.7
  0.0 0.0 copy-start.8
  0.0 13.6 %shard_map.100.part_ref = bf16[32,80,128]{2,1,0:T(8,128)(2,1)} custom-call(bf16[40,32,8192]{2,1,0:T(8,128)(2,1)} %field_ref.3, bf16[8192,256]{1,0:T(8,128)(2,1)} %constant.12.clone.table_ref, bf16[256,256]{1,0:T(8,128)(2,1)} %constant.17.clone.perm_ref), custom_call_target="tpu_custom_call" | custom-call | flops 5368709120 | bytes 25165824 | tf_op jit(solution)/shard_map/pallas_call | solution.py:107
  13.6 0.0 copy-done.1
  13.6 0.0 copy-done.2
  13.6 0.0 copy-done.7
  13.6 0.0 copy-done.8
  13.6 0.0 copy-start
  13.6 1.1 %copy-done = bf16[32,80,128]{2,1,0:T(8,128)(2,1)S(1)} copy-done((bf16[32,80,128]{2,1,0:T(8,128)(2,1)S(1)}, bf16[32,80,128]{2,1,0:T(8,128)(2,1)}, u32[]{:S(2)}) %copy-start) | copy-done | bytes 655384
  14.7 0.0 copy-start.3
  14.7 1.3 %copy-done.3 = bf16[256,2560]{1,0:T(8,128)(2,1)S(1)} copy-done((bf16[256,2560]{1,0:T(8,128)(2,1)S(1)}, bf16[256,2560]{1,0:T(8,128)(2,1)}, u32[]{:S(2)}) %copy-start.3) | copy-done | bytes 1310744
  16.0 0.0 copy-start.4
  16.0 1.3 %copy-done.4 = bf16[256,2560]{1,0:T(8,128)(2,1)S(1)} copy-done((bf16[256,2560]{1,0:T(8,128)(2,1)S(1)}, bf16[256,2560]{1,0:T(8,128)(2,1)}, u32[]{:S(2)}) %copy-start.4) | copy-done | bytes 1310744
  17.3 43.4 %shard_map.101 = (bf16[32,80,128]{2,1,0:T(8,128)(2,1)S(1)}, bf16[256,256]{1,0:T(8,128)(2,1)S(1)}, f32[256,256]{1,0:T(8,128)S(1)}) custom-call(bf16[32,80,128]{2,1,0:T(8,128)(2,1)S(1)} %copy-done, bf16[32,32]{1,0:T(8,128)(2,1)S(1)} %copy-done.7, f32[1,32]{1,0:T(1,128)S(1)} %bitcast.6, bf16[256,2560]{1,0:T(8,128)(2,1)S(1)} %copy-done.4, ...), custom_call_target="tpu_custom_call" | custom-call | tf_op jit(solution)/shard_map/pallas_call | solution.py:399
  60.7 0.0 copy-start.5
  60.7 0.0 copy-start.6
  60.7 0.7 copy.13
  61.5 0.0 copy-done.5
  61.5 0.0 copy-done.6
  61.5 1.3 %reshape.7.half_ref = bf16[40,32,256]{2,1,0:T(8,128)(2,1)} reshape(bf16[40,32,2,128]{3,2,1,0:T(2,128)(2,1)S(1)} %bitcast.7) | data formatting | bytes 1310720 | tf_op jit(solution)/shard_map/reshape | solution.py:466
  62.7 24.7 %shard_map.102 = bf16[40,32,8192]{2,1,0:T(8,128)(2,1)} custom-call(bf16[40,32,8192]{2,1,0:T(8,128)(2,1)} %field_ref.3, bf16[40,32,256]{2,1,0:T(8,128)(2,1)} %reshape.7.half_ref, bf16[256,8192]{1,0:T(8,128)(2,1)} %constant.13.clone.table_ref, bf16[256,256]{1,0:T(8,128)(2,1)} %copy-done.6, f32[256,256]{1,0:T(8,128)} %copy-done.5), custom_call_target="tpu_custom_call" | custom-call | flops 10737418240 | bytes 41943040 | tf_op jit(solution)/shard_map/pallas_call | solution.py:158
Async XLA Ops:
  0.0 13.6 %copy-start.1 = (bf16[2,4,32,32,128]{4,3,2,1,0:T(8,128)(2,1)S(1)}, bf16[2,4,32,32,128]{4,3,2,1,0:T(8,128)(2,1)}, u32[]{:S(2)}) copy-start(bf16[2,4,32,32,128]{4,3,2,1,0:T(8,128)(2,1)} %weight_hbm.1) | copy-start | bytes 6291460
  0.0 13.6 %copy-start.2 = (bf16[2560,256]{1,0:T(8,128)(2,1)S(1)}, bf16[2560,256]{1,0:T(8,128)(2,1)}, u32[]{:S(2)}) copy-start(bf16[2560,256]{1,0:T(8,128)(2,1)} %constant.16.clone.back_hbm) | copy-start | bytes 3932164
  0.0 13.6 %copy-start.7 = (bf16[32,32]{1,0:T(8,128)(2,1)S(1)}, bf16[32,32]{1,0:T(8,128)(2,1)}, u32[]{:S(2)}) copy-start(bf16[32,32]{1,0:T(8,128)(2,1)} %point_ref.1) | copy-start | bytes 6148
  0.0 13.6 %copy-start.8 = (f32[32]{0:T(128)S(1)}, f32[32]{0:T(128)}, u32[]{:S(2)}) copy-start(f32[32]{0:T(128)} %param.13) | copy-start | bytes 388
  13.6 1.1 %copy-start = (bf16[32,80,128]{2,1,0:T(8,128)(2,1)S(1)}, bf16[32,80,128]{2,1,0:T(8,128)(2,1)}, u32[]{:S(2)}) copy-start(bf16[32,80,128]{2,1,0:T(8,128)(2,1)} %shard_map.100.part_ref) | copy-start | bytes 1966084
  14.7 1.3 %copy-start.3 = (bf16[256,2560]{1,0:T(8,128)(2,1)S(1)}, bf16[256,2560]{1,0:T(8,128)(2,1)}, u32[]{:S(2)}) copy-start(bf16[256,2560]{1,0:T(8,128)(2,1)} %constant.15.clone.low_hbm) | copy-start | bytes 3932164
  16.0 1.3 %copy-start.4 = (bf16[256,2560]{1,0:T(8,128)(2,1)S(1)}, bf16[256,2560]{1,0:T(8,128)(2,1)}, u32[]{:S(2)}) copy-start(bf16[256,2560]{1,0:T(8,128)(2,1)} %constant.14.clone.high_hbm) | copy-start | bytes 3932164
  60.7 0.7 copy-start.5
  60.7 0.7 copy-start.6

commit v3 on v2

--- a/solution.py
+++ b/solution.py
@@ -38,10 +38,10 @@
     index = np.arange(modes_x)
     freq = np.where(index < modes_x // 2, index, index - modes_x + length_x)
     phase = phases(freq, np.arange(length_x), length_x)
-    shape = (row_devices, 1, block_x, row_devices, 1, row_count)
+    shape = (row_devices, 1, block_x, row_devices, row_count // CHUNK, 1, CHUNK)
     cosine, sine = np.cos(phase).reshape(shape), np.sin(phase).reshape(shape)
     table = np.concatenate(
-        [np.concatenate([cosine, sine], axis=4), np.concatenate([-sine, cosine], axis=4)], axis=1
+        [np.concatenate([cosine, sine], axis=5), np.concatenate([-sine, cosine], axis=5)], axis=1
     ).reshape(2 * modes_x, 2 * length_x)
     scaled = table * np.float32(1.0 / math.sqrt(length_x))
     high = scaled.astype(BF16)
@@ -54,6 +54,15 @@
     for row in range(rows):
         for channel in range(channels):
             out[channel * rows + row, row * channels + channel] = 1
+    return out
+
+
+def regroup_back(rows, channels):
+    out = np.zeros((2, rows * channels, channels * 2 * rows), BF16)
+    for part in range(2):
+        for row in range(rows):
+            for channel in range(channels):
+                out[part, row * channels + channel, (channel * 2 + part) * rows + row] = 1
     return out
 
 
@@ -92,9 +101,9 @@
                     perm_ref[...], part.astype(jnp.bfloat16), preferred_element_type=jnp.float32
                 )
             moved = moved.reshape(channels, CHUNK, 2 * modes)
-            at = chunk * CHUNK
+            at = 2 * chunk * CHUNK
             ordered[:, at : at + CHUNK, :] = moved[:, :, :modes]
-            ordered[:, rows + at : rows + at + CHUNK, :] = moved[:, :, modes:]
+            ordered[:, at + CHUNK : at + 2 * CHUNK, :] = moved[:, :, modes:]
         out_ref[...] = ordered[...].astype(out_ref.dtype)
 
 
@@ -127,15 +136,27 @@
     )(field, table, jnp.asarray(perm))
 
 
-def inverse_kernel(field_ref, half_ref, table_ref, point_ref, bias_ref, out_ref):
+def inverse_kernel(
+    field_ref, half_ref, perm_ref, table_ref, point_ref, bias_ref, out_ref, ordered
+):
     rows, channels, width = field_ref.shape
     size = CHUNK * channels
     tile = min(width, 256)
+    modes = half_ref.shape[2]
+
+    @pl.when(pl.program_id(0) == 0)
+    def _():
+        for chunk in range(rows // CHUNK):
+            at = 2 * CHUNK * chunk
+            part = half_ref[:, at : at + 2 * CHUNK, :].reshape(2 * size, modes)
+            for side in range(2):
+                moved = jnp.dot(perm_ref[side], part, preferred_element_type=jnp.float32)
+                ordered[chunk, :, side * modes : (side + 1) * modes] = moved.astype(jnp.bfloat16)
 
     @pl.loop(0, rows // CHUNK)
     def _(chunk):
         at = pl.multiple_of(chunk * CHUNK, CHUNK)
-        half = half_ref[pl.ds(at, CHUNK)].reshape(size, half_ref.shape[2])
+        half = ordered[chunk]
         for col in range(0, width, tile):
             values = field_ref[pl.ds(at, CHUNK), :, col : col + tile].reshape(size, tile)
             x = (
@@ -155,25 +176,28 @@
     depth = table.shape[0]
     width = min(cols, 2048)
     size = CHUNK * channels
+    perm = regroup_back(CHUNK, channels)
     return pl.pallas_call(
         inverse_kernel,
         out_shape=jax.ShapeDtypeStruct(field.shape, jnp.bfloat16),
         grid=(cols // width,),
         in_specs=[
             pl.BlockSpec((rows, channels, width), lambda y: (0, 0, y)),
-            pl.BlockSpec((rows, channels, depth), lambda y: (0, 0, 0)),
+            pl.BlockSpec(half.shape, lambda y: (0, 0, 0)),
+            pl.BlockSpec(perm.shape, lambda y: (0, 0, 0)),
             pl.BlockSpec((depth, width), lambda y: (0, y)),
             pl.BlockSpec(point.shape, lambda y: (0, 0)),
             pl.BlockSpec(spread.shape, lambda y: (0, 0)),
         ],
         out_specs=pl.BlockSpec((rows, channels, width), lambda y: (0, 0, y)),
+        scratch_shapes=[pltpu.VMEM((rows // CHUNK, size, depth), jnp.bfloat16)],
         compiler_params=pltpu.CompilerParams(vmem_limit_bytes=60 * 1024 * 1024),
         cost_estimate=pl.CostEstimate(
             flops=2 * rows * channels * cols * (depth + size),
             bytes_accessed=4 * rows * channels * cols,
             transcendentals=rows * channels * cols,
         ),
-    )(field, half, table, point, spread)
+    )(field, half, jnp.asarray(perm), table, point, spread)
 
 
 def mix_modes(spectrum, spec_weight):
@@ -218,10 +242,10 @@
 
 
 def middle_kernel(
-    outer, part_ref, point_ref, bias_ref, high_hbm, low_hbm, back_hbm, weight_hbm,
-    out_ref, point_out, bias_out,
-    high, low, back, weight, part_in, sums, partial_out, partial_in, spec_out, spec_in,
-    mix_out, mix_in, modes_in, half_out, load_sem, send_sem, recv_sem,
+    outer, perm_ref, point_ref, bias_ref, field_hbm, table_hbm, high_hbm, low_hbm, back_hbm,
+    weight_hbm, out_ref, point_out, bias_out,
+    field, table, part_out, high, low, back, weight, part_in, sums, partial_out, partial_in, spec_out, spec_in,
+    mix_out, mix_in, modes_in, half_out, field_sem, table_sem, load_sem, send_sem, recv_sem,
 ):
     me = lax.axis_index("row")
     level, place = me // PLANE, lax.rem(me, PLANE)
@@ -238,8 +262,25 @@
     loads = [
         pltpu.make_async_copy(src, dst, load_sem.at[at]) for at, (src, dst) in enumerate(pairs)
     ]
-    for load in loads:
-        load.start()
+    chunks, slices, size = field.shape[0], field.shape[1], CHUNK * channels
+    width = field.shape[4]
+
+    def load_field(chunk, at):
+        rows = pl.ds(pl.multiple_of(chunk * CHUNK, CHUNK), CHUNK)
+        return pltpu.make_async_copy(
+            field_hbm.at[rows, :, at * width : (at + 1) * width],
+            field.at[chunk, at],
+            field_sem.at[chunk, at],
+        )
+
+    def load_table(at):
+        return pltpu.make_async_copy(
+            table_hbm.at[at * width : (at + 1) * width, :], table.at[at], table_sem.at[at]
+        )
+
+    for at in range(slices):
+        load_table(at).start()
+        load_field(0, at).start()
 
     def in_plane(shift):
         return lax.rem(place + shift, PLANE)
@@ -259,7 +300,6 @@
         to = in_line(shift) * PLANE + place
         pl.semaphore_signal(barrier, inc=1, device_id={"row": to}, device_id_type=MESH)
 
-    size = bias_out.shape[0]
     shape = (size, channels)
     pick = lax.broadcasted_iota(jnp.int32, shape, 0) % channels == lax.broadcasted_iota(
         jnp.int32, shape, 1
@@ -300,7 +340,7 @@
     def plane_copy(phase, piece, shift):
         to = in_plane(shift)
         src, dst = [
-            lambda: (part_ref.at[to * own + piece], part_in.at[piece, place]),
+            lambda: (part_out.at[piece, pl.ds(to * own, own)], part_in.at[place, piece]),
             lambda: (spec_out.at[to], spec_in.at[place]),
             lambda: (mix_out.at[to], mix_in.at[place]),
             lambda: (half_out.at[piece, to], out_ref.at[place * own + piece]),
@@ -320,15 +360,50 @@
         def _(shift):
             getattr(make(phase, piece, shift), act)()
 
-    for piece in range(own):
-        each(plane_copy, 0, piece, PLANE, "start")
-    for piece in range(own):
-        part_in[piece, place] = part_ref[place * own + piece]
+    @pl.loop(0, chunks)
+    def _(chunk):
+        @pl.when(chunk < chunks - 1)
+        def _():
+            for at in range(slices):
+                load_field(chunk + 1, at).start()
+
+        @pl.when(chunk == chunks - 1)
+        def _():
+            for load in loads:
+                load.start()
+
+        total = jnp.zeros((size, 2 * modes), jnp.float32)
+        for at in range(slices):
+
+            @pl.when(chunk == 0)
+            def _():
+                load_table(at).wait()
+
+            load_field(chunk, at).wait()
+            total += jnp.dot(
+                field[chunk, at].reshape(size, width),
+                table[at],
+                preferred_element_type=jnp.float32,
+            )
+        moved = jnp.dot(
+            perm_ref[...], total.astype(jnp.bfloat16), preferred_element_type=jnp.float32
+        )
+        moved = moved.reshape(channels, CHUNK, 2 * modes)
+        moved = jnp.stack([moved[:, :, :modes], moved[:, :, modes:]], axis=1)
+        moved = moved.reshape(channels, 2 * CHUNK, modes).astype(jnp.bfloat16)
+        part_out[chunk] = moved
+        each(plane_copy, 0, chunk, PLANE, "start")
+        part_in[place, chunk] = part_out[chunk, pl.ds(place * own, own)]
+
     loads[0].wait()
     loads[1].wait()
+
+    @pl.loop(0, chunks)
+    def _(chunk):
+        each(plane_copy, 0, chunk, PLANE, "wait_recv")
+
     for piece in range(own):
-        each(plane_copy, 0, piece, PLANE, "wait_recv")
-        part = part_in[piece].reshape(span, modes)
+        part = part_in[:, :, piece].reshape(span, modes)
         spectrum = jnp.dot(high[...], part, preferred_element_type=jnp.float32) + jnp.dot(
             low[...], part, preferred_element_type=jnp.float32
         )
@@ -379,17 +454,21 @@
         out_ref[place * own + piece] = half_out[piece, place]
     for piece in range(own):
         each(plane_copy, 3, piece, PLANE, "wait_recv")
-    for phase in range(4):
-        for piece in range(own if phase in (0, 3) else 1):
+    for phase, count in enumerate((chunks, 1, 1, own)):
+        for piece in range(count):
             each(plane_copy, phase, piece, PLANE, "wait_send")
     for phase in range(2):
         for piece in range(own):
             each(line_copy, phase, piece, outer, "wait_send")
 
 
-def remote_middle(partial_value, spec_weight, point_weight, bias, tables):
+def remote_middle(field, table, spec_weight, point_weight, bias, tables):
     outer = lax.axis_size("row") // PLANE
-    channels, rows, modes = partial_value.shape
+    channels, rows, modes = field.shape[1], 2 * field.shape[0], spec_weight.shape[4]
+    chunks = field.shape[0] // CHUNK
+    width = min(field.shape[2], 2048)
+    slices = field.shape[2] // width
+    perm = regroup(CHUNK, channels)
     block_x = spec_weight.shape[1]
     own = channels // PLANE
     span, depth = PLANE * rows, 2 * block_x
@@ -399,18 +478,21 @@
     return pl.pallas_call(
         functools.partial(middle_kernel, outer),
         out_shape=[
-            jax.ShapeDtypeStruct(partial_value.shape, half),
+            jax.ShapeDtypeStruct((channels, rows, modes), half),
             jax.ShapeDtypeStruct((size, size), half),
             jax.ShapeDtypeStruct((size, size), full),
         ],
-        in_specs=[vmem] * 3 + [pl.BlockSpec(memory_space=pl.ANY)] * 4,
+        in_specs=[vmem] * 3 + [pl.BlockSpec(memory_space=pl.ANY)] * 6,
         out_specs=[vmem] * 3,
         scratch_shapes=[
+            pltpu.VMEM((chunks, slices, CHUNK, channels, width), half),
+            pltpu.VMEM((slices, width, 2 * modes), half),
+            pltpu.VMEM((chunks, channels, 2 * CHUNK, modes), half),
             pltpu.VMEM((outer * PLANE * depth, span), half),
             pltpu.VMEM((outer * PLANE * depth, span), half),
             pltpu.VMEM((span, outer * PLANE * depth), half),
             pltpu.VMEM(spec_weight.shape, half),
-            pltpu.VMEM((own, PLANE, rows, modes), half),
+            pltpu.VMEM((PLANE, chunks, own, 2 * CHUNK, modes), half),
             pltpu.VMEM((own, outer, PLANE * depth, modes), full),
             pltpu.VMEM((own, outer, PLANE * depth, modes), half),
             pltpu.VMEM((own, outer, PLANE * depth, modes), half),
@@ -420,14 +502,16 @@
             pltpu.VMEM((PLANE, own, depth, modes), full),
             pltpu.VMEM((own, outer, PLANE * depth, modes), half),
             pltpu.VMEM((own, PLANE, rows, modes), half),
+            pltpu.SemaphoreType.DMA((chunks, slices)),
+            pltpu.SemaphoreType.DMA((slices,)),
             pltpu.SemaphoreType.DMA((4,)),
-            pltpu.SemaphoreType.DMA((6, own, PLANE)),
-            pltpu.SemaphoreType.DMA((6, own, PLANE)),
+            pltpu.SemaphoreType.DMA((6, max(own, chunks), PLANE)),
+            pltpu.SemaphoreType.DMA((6, max(own, chunks), PLANE)),
         ],
         compiler_params=pltpu.CompilerParams(
-            collective_id=0, has_side_effects=True, vmem_limit_bytes=32 * 1024 * 1024
+            collective_id=0, has_side_effects=True, vmem_limit_bytes=60 * 1024 * 1024
         ),
-    )(partial_value, point_weight, bias[None, :], *tables, spec_weight)
+    )(jnp.asarray(perm), point_weight, bias[None, :], field, table, *tables, spec_weight)
 
 
 def shards(field, spec_weight, point_weight, bias):
@@ -454,16 +538,12 @@
         own = lax.psum_scatter(whole, "col", scatter_dimension=2, tiled=True)
         half = middle(own.astype(jnp.bfloat16), spec_weight, tables)
         half = lax.all_gather(half, "col", axis=2, tiled=True)
+    elif direct:
+        half, point, spread = remote_middle(
+            field, table_y, spec_weight, point_weight, bias, tables
+        )
     else:
-        partial_value = forward(field, table_y, jnp.bfloat16)
-        if direct:
-            half, point, spread = remote_middle(
-                partial_value, spec_weight, point_weight, bias, tables
-            )
-        else:
-            half = middle(partial_value, spec_weight, tables)
-    half = half.reshape(chan_count, 2, row_count, modes_y).transpose(2, 0, 1, 3)
-    half = half.reshape(row_count, chan_count, 2 * modes_y)
+        half = middle(forward(field, table_y, jnp.bfloat16), spec_weight, tables)
     return inverse(field, half, table_back, point, spread)
 
 

time: 87.7 us -> 84.2 us (0.960)
  local copies, waits for them, and re-layouts: 5.69 us -> 0 us
  Pallas kernels: 81.7 us -> 84 us
    pallas_call x1, Pallas kernels: 43.4 us -> 58.3 us  [remote_middle(): pl.pallas_call(functools.partial(middle_kernel, outer), out_shape=[jax.Sh...]
    pallas_call x1 -> x0, Pallas kernels: 13.6 us -> none  [forward(): pl.pallas_call(functools.partial(forward_kernel, steps), out_shape=jax.Sh...]
    unnamed x18 -> x0, local copies, waits for them, and re-layouts: 3.74 us -> none
    reshape x2 -> x0, local copies, waits for them, and re-layouts: 1.95 us -> none  [the longest x1 1.25 us: shards(): half = half.reshape(row_count, chan_count, 2 * modes_y)]
    pallas_call x1, Pallas kernels: 24.7 us -> 25.7 us  [inverse(): pl.pallas_call(inverse_kernel, out_shape=jax.ShapeDtypeStruct(field.shape...]
where the time goes in v3:
time: 84.2 us; the launch traced here: 84 us
  Pallas kernels  84 us (100%)
    pallas_call x1, Pallas kernels, remote_middle(): pl.pallas_call(functools.partial(middle_kernel, outer), out_shape=[jax.Sh...  58.3 us
    pallas_call x1, Pallas kernels, inverse(): pl.pallas_call(inverse_kernel, out_shape=jax.ShapeDtypeStruct(field.shape...  25.7 us

profile of v3, /device:TPU:0, one launch (start us, length us, event | category | flops | bytes accessed | tf_op | source)
XLA Modules:
  0.0 84.0 jit_solution(5339194166871798437)
XLA Ops:
  0.0 58.3 %shard_map.109 = (bf16[32,80,128]{2,1,0:T(8,128)(2,1)}, bf16[256,256]{1,0:T(8,128)(2,1)}, f32[256,256]{1,0:T(8,128)}) custom-call(bf16[256,256]{1,0:T(8,128)(2,1)} %constant.19.clone.perm_ref, bf16[32,32]{1,0:T(8,128)(2,1)} %point_ref.1, f32[1,32]{1,0:T(1,128)} %bitcast.1, bf16[40,32,8192]{2,1,0:T(8,128)(2,1)} %field_ref.1, ...), custom_call_target="tpu_custom_call" | custom-call | tf_op jit(solution)/shard_map/pallas_call | solution.py:478
  58.3 25.7 %shard_map.110 = bf16[40,32,8192]{2,1,0:T(8,128)(2,1)} custom-call(bf16[40,32,8192]{2,1,0:T(8,128)(2,1)} %field_ref.1, bf16[32,80,128]{2,1,0:T(8,128)(2,1)} %get-tuple-element.8.half_ref, bf16[2,256,512]{2,1,0:T(8,128)(2,1)} %constant.20.clone.perm_ref, bf16[256,8192]{1,0:T(8,128)(2,1)} %constant.15.clone.table_ref, ...), custom_call_target="tpu_custom_call" | custom-call | flops 10737418240 | bytes 41943040 | tf_op jit(solution)/shard_map/pallas_call | solution.py:180
